TPU v7x, 128 devices: a whole 4x4x4 slice. The times are simulated.
128 devices in a mesh: band: 4 (over x_hi, core), dom: 32 (over z, y, x_lo).
Axes of the slice: x: 4 (x_hi: 2, x_lo: 2; x = x_hi * 2 + x_lo), y: 4, z: 4, core: 2. Of those that a mesh axis runs over, the one named last changes fastest.
Arguments:
- orbitals: float32 [128, 32, 48, 512], P('dom', None, None, 'band'), may hold values from -6 to 6
- potential: float32 [128, 32, 48], P('dom'), may hold values from -1 to 2
- projectors: float32 [256, 4, 4608], P('dom'), may hold values from -0.09375 to 0.09375
- coupling: float32 [256, 4, 4], P('dom'), may hold values from -4 to 4
- atom_plane: int32 [256], P('dom'), may hold values from 0 to 127, as said below
- projector_count: int32 [256], P('dom'), may hold values from 1 to 4
Outputs:
- filtered: float32 [128, 32, 48, 512], P('dom', None, None, 'band')
- gram: float32 [512, 512], replicated
Inputs may be any that keep to these rules, and one draw needn't show every extreme that they name: `atom_plane`: atom a's first plane lies among the 4 planes of dom index a // 8, that is from (a // 8) * 4 to (a // 8) * 4 + 3; the last atom of each dom index starts on that index's last plane.
All inputs are finite; a program needn't handle non-finite values.
Results may differ from a plain program's by a relative error of at most 0.0003.
Values sent between devices are 32-bit elements; how exact they have to be, the bound alone decides.
A program may use at most 192 MiB of HBM per device.

v0:
```python
import jax
import jax.numpy as jnp
from jax import lax
from jax.sharding import PartitionSpec as P

NORB = 512
HALO = 4
SPAN = 3
MAXPROJ = 4
center_weight = -205.0 / 72.0
side_weights = (8.0 / 5.0, -1.0 / 5.0, 8.0 / 315.0, -1.0 / 560.0)
HIGH = lax.Precision.HIGHEST


def with_halo(value, sides, width):
    for axis, dim in sides:
        peers, length = (lax.axis_size(axis), value.shape[dim])
        up = [(i, (i + 1) % peers) for i in range(peers)]
        down = [(j, i) for i, j in up]
        last = lax.slice_in_dim(value, length - width, length, axis=dim)
        first = lax.slice_in_dim(value, 0, width, axis=dim)
        before = lax.ppermute(last, axis, up)
        after = lax.ppermute(first, axis, down)
        value = jnp.concatenate([before, value, after], axis=dim)
    return value


def passed_along(value, axis, steps):
    count = lax.axis_size(axis)
    pairs = [(source, (source + steps) % count) for source in range(count)]
    return lax.ppermute(value, axis, pairs)


def laplacian(orbital_field, padded, planes):
    total = 3.0 * center_weight * orbital_field
    for offset in range(1, 5):
        weight = side_weights[offset - 1]
        total = total + weight * (
            padded[HALO + offset : HALO + offset + planes]
            + padded[HALO - offset : HALO - offset + planes]
        )
        total = total + weight * (
            jnp.roll(orbital_field, offset, 1) + jnp.roll(orbital_field, -offset, 1)
        )
        total = total + weight * (
            jnp.roll(orbital_field, offset, 2) + jnp.roll(orbital_field, -offset, 2)
        )
    return total


def apply_hamiltonian(orbital_field, potential, layout_pieces):
    planes, side_y, side_z, local_orbs = orbital_field.shape
    beta_full, live_mask, sym_coupling = layout_pieces
    padded = with_halo(orbital_field, (("dom", 0),), HALO)
    extended = padded[HALO : HALO + planes + SPAN - 1].reshape(
        planes + SPAN - 1, side_y * side_z, local_orbs
    )
    correlations = (
        jnp.einsum(
            "ajpc,pco->ajo", beta_full, extended, precision=HIGH, preferred_element_type=jnp.float32
        )
        * live_mask[:, :, None]
    )
    weighted = (
        jnp.einsum(
            "aij,ajo->aio",
            sym_coupling,
            correlations,
            precision=HIGH,
            preferred_element_type=jnp.float32,
        )
        * live_mask[:, :, None]
    )
    contrib = jnp.einsum(
        "ajpc,ajo->pco", beta_full, weighted, precision=HIGH, preferred_element_type=jnp.float32
    )
    contrib = contrib.reshape(planes + SPAN - 1, side_y, side_z, local_orbs)
    arrived = passed_along(contrib[planes:], "dom", 1)
    own_planes = contrib[:planes]
    own_planes = jnp.concatenate([own_planes[: SPAN - 1] + arrived, own_planes[SPAN - 1 :]], axis=0)
    kinetic = -0.5 * laplacian(orbital_field, padded, planes)
    return kinetic + potential[:, :, :, None] * orbital_field + own_planes


def shards(orbitals, potential, projectors, coupling, atom_plane, projector_count):
    planes, side_y, side_z, local_orbs = orbitals.shape
    atom_total = projectors.shape[0]
    first_plane = atom_plane - lax.axis_index("dom") * planes
    plane_ids = jnp.arange(planes + SPAN - 1, dtype=jnp.int32)
    span_ids = jnp.arange(SPAN, dtype=jnp.int32)
    onehot = (
        plane_ids[None, None, :] == first_plane[:, None, None] + span_ids[None, :, None]
    ).astype(jnp.float32)
    beta_split = projectors.reshape(atom_total, MAXPROJ, SPAN, side_y * side_z)
    beta_full = jnp.einsum(
        "akp,ajkc->ajpc", onehot, beta_split, precision=HIGH, preferred_element_type=jnp.float32
    )
    slots = jnp.arange(MAXPROJ, dtype=jnp.int32)
    live_mask = (slots[None, :] < projector_count[:, None]).astype(jnp.float32)
    sym_coupling = 0.5 * (coupling + jnp.transpose(coupling, (0, 2, 1)))
    layout_pieces = (beta_full, live_mask, sym_coupling)
    first = (apply_hamiltonian(orbitals, potential, layout_pieces) - 7.0 * orbitals) / 6.0
    second = (
        2.0 * (apply_hamiltonian(first, potential, layout_pieces) - 7.0 * first) / 6.0 - orbitals
    )
    cells = planes * side_y * side_z
    total_cells = cells * lax.axis_size("dom")
    flat = second.reshape(cells, local_orbs)
    identity = jnp.eye(NORB, dtype=jnp.float32)
    panels = lax.all_gather(flat, "band", axis=1, tiled=True)
    partial_gram = jnp.dot(panels.T, panels, precision=HIGH, preferred_element_type=jnp.float32)
    gram = lax.psum(partial_gram, "dom") * (1.0 / total_cells)
    lower = jnp.linalg.cholesky(gram)
    inverse = jax.scipy.linalg.solve_triangular(lower, identity, lower=True)
    own_rows = lax.dynamic_slice_in_dim(inverse, lax.axis_index("band") * local_orbs, local_orbs, 0)
    result = jnp.dot(panels, own_rows.T, precision=HIGH, preferred_element_type=jnp.float32)
    return (result.reshape(planes, side_y, side_z, local_orbs), gram)


def solution(mesh):
    placed = (
        P("dom", None, None, "band"),
        P("dom", None, None),
        P("dom", None, None),
        P("dom", None, None),
        P("dom"),
        P("dom"),
    )
    return jax.shard_map(
        shards,
        mesh=mesh,
        in_specs=placed,
        out_specs=(P("dom", None, None, "band"), P()),
        check_vma=False,
    )
```

profile of v0, /device:TPU:0, one launch (start us, length us, event | category | flops | bytes accessed | tf_op | source)
XLA Modules:
  0.0 1015.1 jit_solution(8115964120412169199)
XLA Ops:
  8.9 6.0 collective-permute-start
  14.9 2.0 fusion.147
  16.8 2.1 fusion.149
  18.9 2.1 fusion.153
  24.1 2.5 reshape.149
  28.2 2.2 convolution_bitcast_fusion.2
  30.5 3.0 fusion.152
  33.4 2.9 fusion.148
  36.3 3.0 fusion.144
  39.3 3.2 fusion.140
  43.0 41.0 %collective-permute-done.1 = f32[4,32,48,128]{3,2,1,0:T(8,128)} collective-permute-done((f32[4,32,48,128]{3,2,1,0:T(8,128)}, f32[4,32,48,128]{3,2,1,0:T(8,128)}, u32[]{:S(2)}, u32[]{:S(2)}) %collective-permute-start.1) | collective-permute-done | bytes 3145760 | tf_op jit(solution)/shard_map/ppermute | solution.py:22
  84.0 2.2 constant_dynamic-update-slice_fusion.3
  86.7 59.3 %collective-permute-done = f32[4,32,48,128]{3,2,1,0:T(8,128)} collective-permute-done((f32[4,32,48,128]{3,2,1,0:T(8,128)}, f32[4,32,48,128]{3,2,1,0:T(8,128)}, u32[]{:S(2)}, u32[]{:S(2)}) %collective-permute-start) | collective-permute-done | bytes 3145760 | tf_op jit(solution)/shard_map/ppermute | solution.py:23
  146.0 2.1 constant_dynamic-update-slice_fusion
  148.4 3.2 fusion.63
  151.8 7.7 convolution_bitcast_fusion.1
  163.0 3.4 fusion.146
  166.4 3.3 fusion.150
  169.7 3.4 fusion.154
  173.1 27.3 %collective-permute-done.2 = f32[2,32,48,128]{3,2,1,0:T(8,128)S(1)} collective-permute-done((f32[2,32,48,128]{3,2,1,0:T(8,128)S(1)}, f32[2,32,48,128]{3,2,1,0:T(8,128)S(1)}, u32[]{:S(2)}, u32[]{:S(2)}) %collective-permute-start.2) | collective-permute-done | bytes 1572896 | tf_op jit(solution)/shard_map/ppermute | solution.py:31
  201.8 29.0 %broadcast_multiply_fusion = (f32[4,32,48,128]{3,2,1,0:T(8,128)S(1)}, f32[4,32,48,128]{3,2,1,0:T(8,128)}) fusion(f32[4,32,48,128]{3,2,1,0:T(8,128)S(1)} %copy-done, f32[2,32,48,128]{3,2,1,0:T(8,128)} %bitcast.108, f32[2,32,48,128]{3,2,1,0:T(8,128)} %add.258, f32[4,32,48]{2,1,0:T(8,128)} %param.7, f32[4,32,4,128]{3,2,1,0:T(4,128)} %get-tuple-element.95, ...), kind=kLoop, calls=%fused_computation.99 | loop fusion | flops 47972352 | bytes 88104960 | tf_op jit(solution)/shard_map/div | solution.py:102
  238.9 2.9 fusion.136
  241.8 2.9 fusion.132
  244.7 3.0 fusion.128
  247.7 3.1 fusion.124
  250.9 3.2 fusion.126
  254.1 47.8 %collective-permute-done.3 = f32[4,32,48,128]{3,2,1,0:T(8,128)S(1)} collective-permute-done((f32[4,32,48,128]{3,2,1,0:T(8,128)S(1)}, f32[4,32,48,128]{3,2,1,0:T(8,128)S(1)}, u32[]{:S(2)}, u32[]{:S(2)}) %collective-permute-start.3) | collective-permute-done | bytes 3145760 | tf_op jit(solution)/shard_map/ppermute | solution.py:23
  302.5 3.1 fusion.62
  305.7 8.0 convolution_bitcast_fusion
  314.8 3.2 fusion.130
  317.9 3.2 fusion.134
  321.1 3.3 fusion.138
  324.4 77.6 %collective-permute-done.5 = f32[2,32,48,128]{3,2,1,0:T(8,128)S(1)} collective-permute-done((f32[2,32,48,128]{3,2,1,0:T(8,128)S(1)}, f32[2,32,48,128]{3,2,1,0:T(8,128)S(1)}, u32[]{:S(2)}, u32[]{:S(2)}) %collective-permute-start.5) | collective-permute-done | bytes 1572896 | tf_op jit(solution)/shard_map/ppermute | solution.py:31
  405.0 25.2 %multiply_subtract_fusion = f32[4,32,48,128]{3,2,1,0:T(8,128)} fusion(f32[4,32,48,128]{3,2,1,0:T(8,128)S(1)} %copy-done, f32[4,32,48,128]{3,2,1,0:T(8,128)S(1)} %copy-done.2, f32[2,32,48,128]{3,2,1,0:T(8,128)S(1)} %bitcast.109, f32[2,32,48,128]{3,2,1,0:T(8,128)} %add.285, f32[4,32,4,128]{3,2,1,0:T(4,128)} %get-tuple-element.61, ...), kind=kLoop, calls=%fused_computation.97 | loop fusion | flops 53477376 | bytes 72376320 | tf_op jit(solution)/shard_map/sub | solution.py:104
  430.3 85.4 %all-gather.2.cloned.1.call-done = f32[6144,512]{1,0:T(8,128)} async-done(((f32[6144,128]{1,0:T(8,128)}), f32[6144,512]{1,0:T(8,128)}) %all-gather.2.cloned.1.call-update) | async-done | bytes 12582928 | tf_op jit(solution)/shard_map/all_gather | solution.py:110
  515.6 26.2 %fusion.155 = f32[512,512]{0,1:T(8,128)} fusion(f32[6144,512]{1,0:T(8,128)} %all-gather.2.cloned.1.call-done), kind=kOutput, calls=%fused_computation.243 | convolution fusion | flops 19327352832 | bytes 13631488 | tf_op jit(solution)/shard_map/dot_general | solution.py:111
  543.8 307.9 %all-reduce.3.cloned.1.call-done = f32[512,512]{0,1:T(8,128)} async-done(((f32[512,512]{0,1:T(8,128)}), f32[512,512]{0,1:T(8,128)}) %all-reduce.3.cloned.1.call-update) | async-done | bytes 1048592 | tf_op jit(solution)/shard_map/psum | solution.py:112
  853.7 11.7 %cholesky.104 = f32[128,128]{1,0:T(8,128)S(1)} custom-call(f32[128,128]{1,0:T(8,128)S(1)} %cholesky.266), custom_call_target="Cholesky" | custom-call | tf_op jit(solution)/shard_map/jit(cholesky)/cholesky | solution.py:113
  865.6 9.8 custom-call.31
  877.1 11.7 %cholesky.217 = f32[128,128]{1,0:T(8,128)S(1)} custom-call(f32[128,128]{1,0:T(8,128)S(1)} %cholesky.270), custom_call_target="Cholesky" | custom-call | tf_op jit(solution)/shard_map/jit(cholesky)/cholesky | solution.py:113
  888.9 10.0 custom-call.32
  900.5 11.7 %cholesky.238 = f32[128,128]{1,0:T(8,128)S(1)} custom-call(f32[128,128]{1,0:T(8,128)S(1)} %cholesky.275), custom_call_target="Cholesky" | custom-call | tf_op jit(solution)/shard_map/jit(cholesky)/cholesky | solution.py:113
  912.9 9.8 custom-call.33
  924.1 11.9 %cholesky.255 = f32[128,128]{1,0:T(8,128)S(1)} custom-call(f32[128,128]{1,0:T(8,128)S(1)} %convolution_subtract_fusion.5), custom_call_target="Cholesky" | custom-call | tf_op jit(solution)/shard_map/jit(cholesky)/cholesky | solution.py:113
  940.0 10.1 while.1
  948.2 1.9 bitcast_dynamic-update-slice_fusion.2
  950.1 40.1 %custom-call.34 = f32[4,128,128]{1,2,0:T(8,128)S(1)} custom-call(f32[4,128,128]{2,1,0:T(8,128)} %get-tuple-element.9), custom_call_target="InvertDiagBlocksLowerTriangular" | custom-call | tf_op jit(solution)/shard_map/jit(_solve_triangular)/triangular_solve | solution.py:114
  994.1 13.8 %fusion.81 = f32[6144,128]{1,0:T(8,128)} fusion(f32[6144,512]{1,0:T(8,128)} %all-gather.2.cloned.1.call-done, s32[]{:T(128)S(6)} %select_n.8, f32[128,512]{1,0:T(8,128)S(1)} %fusion.84, f32[128,512]{1,0:T(8,128)S(1)} %fusion.96, f32[128,512]{1,0:T(8,128)S(1)} %fusion.94, f32[128,512]{1,0:T(8,128)S(1)} %fusion.93), kind=kOutput, calls=%fused_computation.138 | convolution fusion | flops 4832034816 | bytes 16777220 | tf_op jit(solution)/shard_map/dot_general | solution.py:116
  (111 shorter events, 48.4 us)
Async XLA Ops:
  7.2 13.9 %copy-start = (f32[4,32,48,128]{3,2,1,0:T(8,128)S(1)}, f32[4,32,48,128]{3,2,1,0:T(8,128)}, u32[]{:S(2)}) copy-start(f32[4,32,48,128]{3,2,1,0:T(8,128)} %param.6) | copy-start | bytes 9437188
  7.2 508.5 %all-gather.2.cloned.1.call-start = ((), (), s32[]{:S(2)}) async-start(), calls=%async_computation | async-start | bytes 15728640 | tf_op jit(solution)/shard_map/all_gather | solution.py:110
  7.2 76.8 %collective-permute-start.1 = (f32[4,32,48,128]{3,2,1,0:T(8,128)}, f32[4,32,48,128]{3,2,1,0:T(8,128)}, u32[]{:S(2)}, u32[]{:S(2)}) collective-permute-start(f32[4,32,48,128]{3,2,1,0:T(8,128)} %param.6), channel_id=1, source_target_pairs={{0,1},{1,2},{2,3},{3,4},{4,5},{5,6},{6,7},{7,8},{8,9},{9,10},{10,1... | collective-permute-start | bytes 9437192 | tf_op jit(solution)/shard_map/ppermute | solution.py:22
  8.9 137.1 %collective-permute-start = (f32[4,32,48,128]{3,2,1,0:T(8,128)}, f32[4,32,48,128]{3,2,1,0:T(8,128)}, u32[]{:S(2)}, u32[]{:S(2)}) collective-permute-start(f32[4,32,48,128]{3,2,1,0:T(8,128)} %param.6), channel_id=1, source_target_pairs={{1,0},{2,1},{3,2},{4,3},{5,4},{6,5},{7,6},{8,7},{9,8},{10,9},{11,1... | collective-permute-start | bytes 9437192 | tf_op jit(solution)/shard_map/ppermute | solution.py:23
  14.9 11.7 %copy-start.12 = (f32[8,4,4]{0,2,1:T(4,128)S(1)}, f32[8,4,4]{0,2,1:T(4,128)}, u32[]{:S(2)}) copy-start(f32[8,4,4]{0,2,1:T(4,128)} %param.9) | copy-start | bytes 1540
  14.9 11.8 %copy-start.13 = (s32[8]{0:T(128)S(1)}, s32[8]{0:T(128)}, u32[]{:S(2)}) copy-start(s32[8]{0:T(128)} %param.10) | copy-start | bytes 100
  30.4 121.3 %copy-start.3 = (f32[8,4,6,1536]{3,2,1,0:T(8,128)}, f32[8,4,6,1536]{3,2,1,0:T(8,128)S(1)}, u32[]{:S(2)}) copy-start(f32[8,4,6,1536]{3,2,1,0:T(8,128)S(1)} %convolution_bitcast_fusion.2) | copy-start | bytes 3538948
  86.7 64.9 %copy-start.1 = (f32[8,32,48,128]{3,2,1,0:T(8,128)}, f32[8,32,48,128]{3,2,1,0:T(8,128)S(1)}, u32[]{:S(2)}) copy-start(f32[8,32,48,128]{3,2,1,0:T(8,128)S(1)} %get-tuple-element.80) | copy-start | bytes 18874372
  159.5 2.9 copy-start.11
  160.9 39.5 %collective-permute-start.2 = (f32[2,32,48,128]{3,2,1,0:T(8,128)S(1)}, f32[2,32,48,128]{3,2,1,0:T(8,128)S(1)}, u32[]{:S(2)}, u32[]{:S(2)}) collective-permute-start(f32[2,32,48,128]{3,2,1,0:T(8,128)S(1)} %bitcast.112), channel_id=1, source_target_pairs={{0,1},{1,2},{2,3},{3,4},{4,5},{5,6},{6,7},{7,8},{8,9},{9,10},{10,1... | collective-permute-start | bytes 4718600 | tf_op jit(solution)/shard_map/ppermute | solution.py:31
  173.1 28.7 %copy-start.10 = (f32[4,1,48,128]{3,2,1,0:T(8,128)S(1)}, f32[4,1,48,128]{3,2,1,0:T(8,128)}, u32[]{:S(2)}) copy-start(f32[4,1,48,128]{3,2,1,0:T(8,128)} %get-tuple-element.64) | copy-start | bytes 294916
  230.8 71.1 %collective-permute-start.3 = (f32[4,32,48,128]{3,2,1,0:T(8,128)S(1)}, f32[4,32,48,128]{3,2,1,0:T(8,128)S(1)}, u32[]{:S(2)}, u32[]{:S(2)}) collective-permute-start(f32[4,32,48,128]{3,2,1,0:T(8,128)S(1)} %get-tuple-element.22), channel_id=1, source_target_pairs={{1,0},{2,1},{3,2},{4,3},{5,4},{6,5},{7,6},{8,7},{9,8},{10,9},{11,1... | collective-permute-start | bytes 9437192 | tf_op jit(solution)/shard_map/ppermute | solution.py:23
  234.3 169.0 %collective-permute-start.4 = (f32[4,32,48,128]{3,2,1,0:T(8,128)S(1)}, f32[4,32,48,128]{3,2,1,0:T(8,128)S(1)}, u32[]{:S(2)}, u32[]{:S(2)}) collective-permute-start(f32[4,32,48,128]{3,2,1,0:T(8,128)S(1)} %get-tuple-element.22), channel_id=1, source_target_pairs={{0,1},{1,2},{2,3},{3,4},{4,5},{5,6},{6,7},{7,8},{8,9},{9,10},{10,1... | collective-permute-start | bytes 9437192 | tf_op jit(solution)/shard_map/ppermute | solution.py:22
  254.1 48.4 %copy-start.4 = (f32[8,4,6,1536]{3,2,1,0:T(8,128)S(1)}, f32[8,4,6,1536]{3,2,1,0:T(8,128)}, u32[]{:S(2)}) copy-start(f32[8,4,6,1536]{3,2,1,0:T(8,128)} %copy-done.3) | copy-start | bytes 3538948
  314.0 88.0 %collective-permute-start.5 = (f32[2,32,48,128]{3,2,1,0:T(8,128)S(1)}, f32[2,32,48,128]{3,2,1,0:T(8,128)S(1)}, u32[]{:S(2)}, u32[]{:S(2)}) collective-permute-start(f32[2,32,48,128]{3,2,1,0:T(8,128)S(1)} %bitcast.111), channel_id=1, source_target_pairs={{0,1},{1,2},{2,3},{3,4},{4,5},{5,6},{6,7},{7,8},{8,9},{9,10},{10,1... | collective-permute-start | bytes 4718600 | tf_op jit(solution)/shard_map/ppermute | solution.py:31
  324.4 80.6 %copy-start.2 = (f32[4,32,48,128]{3,2,1,0:T(8,128)S(1)}, f32[4,32,48,128]{3,2,1,0:T(8,128)}, u32[]{:S(2)}) copy-start(f32[4,32,48,128]{3,2,1,0:T(8,128)} %get-tuple-element.23) | copy-start | bytes 9437188
  403.3 1.6 copy-start.8
  430.2 421.5 %all-reduce.3.cloned.1.call-start = ((), (), s32[]{:S(2)}) async-start(), calls=%async_computation.1 | async-start | bytes 2097152 | tf_op jit(solution)/shard_map/psum | solution.py:112
  851.7 1.8 copy-start.6
  853.4 45.7 %copy-start.5 = (f32[512,512]{1,0:T(8,128)}, f32[512,512]{1,0:T(8,128)S(1)}, u32[]{:S(2)}) copy-start(f32[512,512]{1,0:T(8,128)S(1)} %copy.20) | copy-start | bytes 3145732
  853.7 22.0 %copy-start.9 = (f32[512,512]{1,0:T(8,128)}, f32[512,512]{1,0:T(8,128)S(1)}, u32[]{:S(2)}) copy-start(f32[512,512]{1,0:T(8,128)S(1)} %fusion.64) | copy-start | bytes 3145732
  875.8 115.6 %copy-start.7 = (f32[512,512]{1,0:T(8,128)S(1)}, f32[512,512]{1,0:T(8,128)}, u32[]{:S(2)}) copy-start(f32[512,512]{1,0:T(8,128)} %fusion.77) | copy-start | bytes 3145732
Sparse Core Ops, SparseCore 0:
  430.3 85.2 all-gather.1
  542.0 309.6 all-reduce.2
where the time goes:
time: 1020 us
  waiting for transfers between devices  646 us (63%)
  other arithmetic  181 us (18%)
  local copies, waits for them, and re-layouts  85.5 us (8%)
  matrix products  72.9 us (7%)
  between operations  17.4 us (2%)
  starting transfers between devices  11.6 us (1%)
    psum x1, waiting for transfers between devices, shards(): gram = lax.psum(partial_gram, 'dom') * (1.0 / total_cells)  308 us
    ppermute x2, waiting for transfers between devices, with_halo(): after = lax.ppermute(first, axis, down)  107 us
    ppermute x2, waiting for transfers between devices, passed_along(): return lax.ppermute(value, axis, pairs)  105 us
    all_gather x1, waiting for transfers between devices, shards(): panels = lax.all_gather(flat, 'band', axis=1, tiled=True)  85.4 us
    another operation x14, other arithmetic, shards(): lower = jnp.linalg.cholesky(gram)  78.8 us
    ppermute x2, waiting for transfers between devices, with_halo(): before = lax.ppermute(last, axis, up)  41 us
    another operation x3, other arithmetic, shards(): inverse = jax.scipy.linalg.solve_triangular(lower, identity, lower=True)  40.3 us
    slice x16, local copies, waits for them, and re-layouts, laplacian(): jnp.roll(orbital_field, offset, 2) + jnp.roll(orbital_field, -offset, 2)  32.4 us
  transfers between devices with their start and end apart: 8, of which 7 were waited for; matrix products, arithmetic and copies ran while one was open for 9% of the time, Pallas kernels for 0%

commit v1 on v0

--- a/solution.py
+++ b/solution.py
@@ -107,7 +107,9 @@
     total_cells = cells * lax.axis_size("dom")
     flat = second.reshape(cells, local_orbs)
     identity = jnp.eye(NORB, dtype=jnp.float32)
-    panels = lax.all_gather(flat, "band", axis=1, tiled=True)
+    panels = jnp.concatenate(
+        lax.all_to_all(jnp.stack([flat] * lax.axis_size("band")), "band", 0, 0), axis=1
+    )
     partial_gram = jnp.dot(panels.T, panels, precision=HIGH, preferred_element_type=jnp.float32)
     gram = lax.psum(partial_gram, "dom") * (1.0 / total_cells)
     lower = jnp.linalg.cholesky(gram)

time: 1020 us -> 1090 us (1.069)
  blocking collectives: 0 us -> 144 us
  waiting for transfers between devices: 646 us -> 525 us
  local copies, waits for them, and re-layouts: 85.5 us -> 133 us
    all_to_all x0 -> x1, blocking collectives: none -> 144 us  [shards(): lax.all_to_all(jnp.stack([flat] * lax.axis_size('band')), 'band', 0, 0)]
    all_gather x1 -> x0, waiting for transfers between devices: 85.4 us -> none  [shards(): panels = lax.all_gather(flat, 'band', axis=1, tiled=True)]
    psum x1, waiting for transfers between devices: 308 us -> 272 us  [shards(): gram = lax.psum(partial_gram, 'dom') * (1.0 / total_cells)]
    reshape x0 -> x1, local copies, waits for them, and re-layouts: none -> 16.4 us  [shards(): jnp.concatenate(lax.all_to_all(jnp.stack([flat] * lax.axis_size('band')),...]
    dot_general x0 -> x1, local copies, waits for them, and re-layouts: none -> 15.3 us  [shards(): jnp.dot(panels, own_rows.T, precision=HIGH, preferred_element_type=jnp.fl...]
    all_to_all x0 -> x1, local copies, waits for them, and re-layouts: none -> 12.6 us  [shards(): lax.all_to_all(jnp.stack([flat] * lax.axis_size('band')), 'band', 0, 0)]
  transfers between devices with their start and end apart: 8 -> 7, of which waited for: 7 -> 6; matrix products, arithmetic and copies ran while one was open for 9% -> 11% of each run, Pallas kernels for 0% -> 0%
where the time goes in v1:
time: 1090 us; the launch traced here: 1080 us
  waiting for transfers between devices  525 us (48%)
  other arithmetic  181 us (17%)
  blocking collectives  144 us (13%)
  local copies, waits for them, and re-layouts  133 us (12%)
  matrix products  71.1 us (7%)
  between operations  17.3 us (2%)
  starting transfers between devices  11.5 us (1%)
    psum x1, waiting for transfers between devices, shards(): gram = lax.psum(partial_gram, 'dom') * (1.0 / total_cells)  272 us
    all_to_all x1, blocking collectives, shards(): lax.all_to_all(jnp.stack([flat] * lax.axis_size('band')), 'band', 0, 0)  144 us
    ppermute x2, waiting for transfers between devices, with_halo(): after = lax.ppermute(first, axis, down)  107 us
    ppermute x2, waiting for transfers between devices, passed_along(): return lax.ppermute(value, axis, pairs)  105 us
    another operation x14, other arithmetic, shards(): lower = jnp.linalg.cholesky(gram)  79 us
    ppermute x2, waiting for transfers between devices, with_halo(): before = lax.ppermute(last, axis, up)  41.1 us
    another operation x3, other arithmetic, shards(): inverse = jax.scipy.linalg.solve_triangular(lower, identity, lower=True)  40.3 us
    slice x16, local copies, waits for them, and re-layouts, laplacian(): jnp.roll(orbital_field, offset, 2) + jnp.roll(orbital_field, -offset, 2)  32.5 us
  transfers between devices with their start and end apart: 7, of which 6 were waited for; matrix products, arithmetic and copies ran while one was open for 11% of the time, Pallas kernels for 0%

profile of v1, /device:TPU:0, one launch (start us, length us, event | category | flops | bytes accessed | tf_op | source)
XLA Modules:
  0.0 1083.4 jit_solution(12465063279801248917)
XLA Ops:
  8.9 6.0 collective-permute-start
  24.1 2.5 reshape.155
  28.2 2.2 convolution_bitcast_fusion.2
  30.5 2.9 fusion.153
  33.4 2.9 fusion.149
  36.3 3.0 fusion.145
  39.3 3.2 fusion.141
  43.0 41.1 %collective-permute-done.1 = f32[4,32,48,128]{3,2,1,0:T(8,128)} collective-permute-done((f32[4,32,48,128]{3,2,1,0:T(8,128)}, f32[4,32,48,128]{3,2,1,0:T(8,128)}, u32[]{:S(2)}, u32[]{:S(2)}) %collective-permute-start.1) | collective-permute-done | bytes 3145760 | tf_op jit(solution)/shard_map/ppermute | solution.py:22
  84.0 2.2 constant_dynamic-update-slice_fusion.3
  86.7 59.3 %collective-permute-done = f32[4,32,48,128]{3,2,1,0:T(8,128)} collective-permute-done((f32[4,32,48,128]{3,2,1,0:T(8,128)}, f32[4,32,48,128]{3,2,1,0:T(8,128)}, u32[]{:S(2)}, u32[]{:S(2)}) %collective-permute-start) | collective-permute-done | bytes 3145760 | tf_op jit(solution)/shard_map/ppermute | solution.py:23
  146.0 2.1 constant_dynamic-update-slice_fusion
  148.4 3.2 fusion.63
  151.8 7.7 convolution_bitcast_fusion.1
  163.1 3.4 fusion.143
  166.4 3.3 fusion.147
  169.8 3.4 fusion.151
  173.1 27.3 %collective-permute-done.2 = f32[2,32,48,128]{3,2,1,0:T(8,128)S(1)} collective-permute-done((f32[2,32,48,128]{3,2,1,0:T(8,128)S(1)}, f32[2,32,48,128]{3,2,1,0:T(8,128)S(1)}, u32[]{:S(2)}, u32[]{:S(2)}) %collective-permute-start.2) | collective-permute-done | bytes 1572896 | tf_op jit(solution)/shard_map/ppermute | solution.py:31
  201.8 28.7 %broadcast_multiply_fusion = (f32[4,32,48,128]{3,2,1,0:T(8,128)S(1)}, f32[4,32,48,128]{3,2,1,0:T(8,128)}) fusion(f32[4,32,48,128]{3,2,1,0:T(8,128)S(1)} %copy-done, f32[2,32,48,128]{3,2,1,0:T(8,128)} %bitcast.118, f32[2,32,48,128]{3,2,1,0:T(8,128)} %add.258, f32[4,32,48]{2,1,0:T(8,128)} %param.7, f32[4,32,4,128]{3,2,1,0:T(4,128)} %get-tuple-element.99, ...), kind=kLoop, calls=%fused_computation.99 | loop fusion | flops 47972352 | bytes 88104960 | tf_op jit(solution)/shard_map/div | solution.py:102
  238.6 2.8 fusion.137
  241.4 2.9 fusion.133
  244.3 3.0 fusion.129
  247.3 3.1 fusion.125
  250.3 3.2 fusion.127
  253.5 48.1 %collective-permute-done.3 = f32[4,32,48,128]{3,2,1,0:T(8,128)S(1)} collective-permute-done((f32[4,32,48,128]{3,2,1,0:T(8,128)S(1)}, f32[4,32,48,128]{3,2,1,0:T(8,128)S(1)}, u32[]{:S(2)}, u32[]{:S(2)}) %collective-permute-start.3) | collective-permute-done | bytes 3145760 | tf_op jit(solution)/shard_map/ppermute | solution.py:23
  302.1 3.1 fusion.62
  305.4 7.9 convolution_bitcast_fusion
  314.4 3.2 fusion.131
  317.6 3.2 fusion.135
  320.8 3.3 fusion.139
  324.1 77.6 %collective-permute-done.5 = f32[2,32,48,128]{3,2,1,0:T(8,128)S(1)} collective-permute-done((f32[2,32,48,128]{3,2,1,0:T(8,128)S(1)}, f32[2,32,48,128]{3,2,1,0:T(8,128)S(1)}, u32[]{:S(2)}, u32[]{:S(2)}) %collective-permute-start.5) | collective-permute-done | bytes 1572896 | tf_op jit(solution)/shard_map/ppermute | solution.py:31
  404.7 25.3 %multiply_subtract_fusion = f32[4,32,48,128]{3,2,1,0:T(8,128)} fusion(f32[4,32,48,128]{3,2,1,0:T(8,128)S(1)} %copy-done, f32[4,32,48,128]{3,2,1,0:T(8,128)S(1)} %copy-done.2, f32[2,32,48,128]{3,2,1,0:T(8,128)S(1)} %bitcast.119, f32[2,32,48,128]{3,2,1,0:T(8,128)} %add.285, f32[4,32,4,128]{3,2,1,0:T(4,128)} %get-tuple-element.65, ...), kind=kLoop, calls=%fused_computation.97 | loop fusion | flops 53477376 | bytes 72376320 | tf_op jit(solution)/shard_map/sub | solution.py:104
  429.9 2.7 stack.3
  432.6 143.8 %all_to_all.5 = f32[4,6144,128]{2,1,0:T(8,128)} all-to-all(f32[4,6144,128]{2,1,0:T(8,128)S(1)} %stack.3), channel_id=1, replica_groups=mesh['band'=4,'dom'=32] {'band'}, dimensions={0} | all-to-all | bytes 25165824 | tf_op jit(solution)/shard_map/all_to_all | solution.py:111
  576.4 12.6 %copy.52 = f32[4,6144,128]{1,2,0:T(8,128)} copy(f32[4,6144,128]{2,1,0:T(8,128)} %all_to_all.5) | data formatting | bytes 25165824 | tf_op jit(solution)/shard_map/all_to_all | solution.py:111
  589.1 24.4 %fusion.156 = f32[512,512]{0,1:T(8,128)} fusion(f32[6144,512]{0,1:T(8,128)} %bitcast.111), kind=kOutput, calls=%fused_computation.244 | convolution fusion | flops 19327352832 | bytes 13631488 | tf_op jit(solution)/shard_map/dot_general | solution.py:113
  615.4 16.4 %copy.53 = f32[6144,4,128]{2,1,0:T(4,128)} copy(f32[6144,4,128]{2,0,1:T(8,128)} %bitcast.112) | data formatting | bytes 25165824 | tf_op jit(solution)/shard_map/reshape | solution.py:110
  631.8 15.3 %dot_general.36 = f32[4,32,48,512]{3,2,1,0:T(8,128)} reshape(f32[6144,4,128]{2,1,0:T(4,128)} %copy.53) | data formatting | bytes 25165824 | tf_op jit(solution)/shard_map/dot_general | solution.py:118
  647.2 271.8 %all-reduce.3.cloned.1.call-done = f32[512,512]{0,1:T(8,128)} async-done(((f32[512,512]{0,1:T(8,128)}), f32[512,512]{0,1:T(8,128)}) %all-reduce.3.cloned.1.call-update) | async-done | bytes 1048592 | tf_op jit(solution)/shard_map/psum | solution.py:114
  921.0 11.7 %cholesky.104 = f32[128,128]{1,0:T(8,128)S(1)} custom-call(f32[128,128]{1,0:T(8,128)S(1)} %cholesky.266), custom_call_target="Cholesky" | custom-call | tf_op jit(solution)/shard_map/jit(cholesky)/cholesky | solution.py:115
  932.9 9.8 custom-call.31
  944.4 11.7 %cholesky.217 = f32[128,128]{1,0:T(8,128)S(1)} custom-call(f32[128,128]{1,0:T(8,128)S(1)} %cholesky.270), custom_call_target="Cholesky" | custom-call | tf_op jit(solution)/shard_map/jit(cholesky)/cholesky | solution.py:115
  956.2 10.2 custom-call.32
  967.9 11.7 %cholesky.238 = f32[128,128]{1,0:T(8,128)S(1)} custom-call(f32[128,128]{1,0:T(8,128)S(1)} %cholesky.275), custom_call_target="Cholesky" | custom-call | tf_op jit(solution)/shard_map/jit(cholesky)/cholesky | solution.py:115
  980.4 9.8 custom-call.33
  991.7 11.7 %cholesky.255 = f32[128,128]{1,0:T(8,128)S(1)} custom-call(f32[128,128]{1,0:T(8,128)S(1)} %convolution_subtract_fusion.5), custom_call_target="Cholesky" | custom-call | tf_op jit(solution)/shard_map/jit(cholesky)/cholesky | solution.py:115
  1007.6 10.9 %while.1 = (s32[]{:T(128)}, f32[512,512]{1,0:T(8,128)S(1)}, s32[4,2]{0,1:T(2,128)S(1)}, f32[4,128,128]{2,1,0:T(8,128)}, s32[]{:T(128)}) while((s32[]{:T(128)}, f32[512,512]{1,0:T(8,128)S(1)}, s32[4,2]{0,1:T(2,128)S(1)}, f32[4,128,128]{2,1,0:T(8,128)}, s32[]{:T(128)}) %tuple.73), condition=%wide.while_cond, body=%wide.while_body.sunk | while | flops 2 | bytes 132705 | solution.py:116
  1018.6 40.1 %custom-call.34 = f32[4,128,128]{1,2,0:T(8,128)S(1)} custom-call(f32[4,128,128]{2,1,0:T(8,128)} %get-tuple-element.9), custom_call_target="InvertDiagBlocksLowerTriangular" | custom-call | tf_op jit(solution)/shard_map/jit(_solve_triangular)/triangular_solve | solution.py:116
  1062.5 13.8 %fusion.82 = f32[4,32,48,128]{3,2,1,0:T(8,128)} fusion(f32[4,32,48,512]{3,2,1,0:T(8,128)} %dot_general.36, s32[]{:T(128)S(6)} %select_n.8, f32[128,512]{1,0:T(8,128)S(1)} %fusion.85, f32[128,512]{1,0:T(8,128)S(1)} %fusion.97, f32[128,512]{1,0:T(8,128)S(1)} %fusion.95, f32[128,512]{1,0:T(8,128)S(1)} %fusion.94), kind=kOutput, calls=%fused_computation.139 | convolution fusion | flops 4832034816 | bytes 16777220 | tf_op jit(solution)/shard_map/dot_general | solution.py:118
  (113 shorter events, 57.7 us)
Async XLA Ops:
  7.2 13.9 %copy-start = (f32[4,32,48,128]{3,2,1,0:T(8,128)S(1)}, f32[4,32,48,128]{3,2,1,0:T(8,128)}, u32[]{:S(2)}) copy-start(f32[4,32,48,128]{3,2,1,0:T(8,128)} %param.6) | copy-start | bytes 9437188
  7.2 911.8 %all-reduce.3.cloned.1.call-start = ((), (), s32[]{:S(2)}) async-start(), calls=%async_computation.1 | async-start | bytes 2097152 | tf_op jit(solution)/shard_map/psum | solution.py:114
  7.2 76.8 %collective-permute-start.1 = (f32[4,32,48,128]{3,2,1,0:T(8,128)}, f32[4,32,48,128]{3,2,1,0:T(8,128)}, u32[]{:S(2)}, u32[]{:S(2)}) collective-permute-start(f32[4,32,48,128]{3,2,1,0:T(8,128)} %param.6), channel_id=1, source_target_pairs={{0,1},{1,2},{2,3},{3,4},{4,5},{5,6},{6,7},{7,8},{8,9},{9,10},{10,1... | collective-permute-start | bytes 9437192 | tf_op jit(solution)/shard_map/ppermute | solution.py:22
  8.9 137.1 %collective-permute-start = (f32[4,32,48,128]{3,2,1,0:T(8,128)}, f32[4,32,48,128]{3,2,1,0:T(8,128)}, u32[]{:S(2)}, u32[]{:S(2)}) collective-permute-start(f32[4,32,48,128]{3,2,1,0:T(8,128)} %param.6), channel_id=1, source_target_pairs={{1,0},{2,1},{3,2},{4,3},{5,4},{6,5},{7,6},{8,7},{9,8},{10,9},{11,1... | collective-permute-start | bytes 9437192 | tf_op jit(solution)/shard_map/ppermute | solution.py:23
  14.9 11.7 %copy-start.12 = (f32[8,4,4]{0,2,1:T(4,128)S(1)}, f32[8,4,4]{0,2,1:T(4,128)}, u32[]{:S(2)}) copy-start(f32[8,4,4]{0,2,1:T(4,128)} %param.9) | copy-start | bytes 1540
  14.9 11.8 %copy-start.13 = (s32[8]{0:T(128)S(1)}, s32[8]{0:T(128)}, u32[]{:S(2)}) copy-start(s32[8]{0:T(128)} %param.10) | copy-start | bytes 100
  30.5 121.3 %copy-start.3 = (f32[8,4,6,1536]{3,2,1,0:T(8,128)}, f32[8,4,6,1536]{3,2,1,0:T(8,128)S(1)}, u32[]{:S(2)}) copy-start(f32[8,4,6,1536]{3,2,1,0:T(8,128)S(1)} %convolution_bitcast_fusion.2) | copy-start | bytes 3538948
  86.7 61.4 %copy-start.1 = (f32[8,32,48,128]{3,2,1,0:T(8,128)}, f32[8,32,48,128]{3,2,1,0:T(8,128)S(1)}, u32[]{:S(2)}) copy-start(f32[8,32,48,128]{3,2,1,0:T(8,128)S(1)} %get-tuple-element.84) | copy-start | bytes 18874372
  159.5 2.9 copy-start.11
  160.9 39.5 %collective-permute-start.2 = (f32[2,32,48,128]{3,2,1,0:T(8,128)S(1)}, f32[2,32,48,128]{3,2,1,0:T(8,128)S(1)}, u32[]{:S(2)}, u32[]{:S(2)}) collective-permute-start(f32[2,32,48,128]{3,2,1,0:T(8,128)S(1)} %bitcast.121), channel_id=1, source_target_pairs={{0,1},{1,2},{2,3},{3,4},{4,5},{5,6},{6,7},{7,8},{8,9},{9,10},{10,1... | collective-permute-start | bytes 4718600 | tf_op jit(solution)/shard_map/ppermute | solution.py:31
  173.1 28.7 %copy-start.10 = (f32[4,1,48,128]{3,2,1,0:T(8,128)S(1)}, f32[4,1,48,128]{3,2,1,0:T(8,128)}, u32[]{:S(2)}) copy-start(f32[4,1,48,128]{3,2,1,0:T(8,128)} %get-tuple-element.68) | copy-start | bytes 294916
  230.5 71.1 %collective-permute-start.3 = (f32[4,32,48,128]{3,2,1,0:T(8,128)S(1)}, f32[4,32,48,128]{3,2,1,0:T(8,128)S(1)}, u32[]{:S(2)}, u32[]{:S(2)}) collective-permute-start(f32[4,32,48,128]{3,2,1,0:T(8,128)S(1)} %get-tuple-element.26), channel_id=1, source_target_pairs={{1,0},{2,1},{3,2},{4,3},{5,4},{6,5},{7,6},{8,7},{9,8},{10,9},{11,1... | collective-permute-start | bytes 9437192 | tf_op jit(solution)/shard_map/ppermute | solution.py:23
  234.0 169.0 %collective-permute-start.4 = (f32[4,32,48,128]{3,2,1,0:T(8,128)S(1)}, f32[4,32,48,128]{3,2,1,0:T(8,128)S(1)}, u32[]{:S(2)}, u32[]{:S(2)}) collective-permute-start(f32[4,32,48,128]{3,2,1,0:T(8,128)S(1)} %get-tuple-element.26), channel_id=1, source_target_pairs={{0,1},{1,2},{2,3},{3,4},{4,5},{5,6},{6,7},{7,8},{8,9},{9,10},{10,1... | collective-permute-start | bytes 9437192 | tf_op jit(solution)/shard_map/ppermute | solution.py:22
  253.5 48.6 %copy-start.4 = (f32[8,4,6,1536]{3,2,1,0:T(8,128)S(1)}, f32[8,4,6,1536]{3,2,1,0:T(8,128)}, u32[]{:S(2)}) copy-start(f32[8,4,6,1536]{3,2,1,0:T(8,128)} %copy-done.3) | copy-start | bytes 3538948
  313.7 88.0 %collective-permute-start.5 = (f32[2,32,48,128]{3,2,1,0:T(8,128)S(1)}, f32[2,32,48,128]{3,2,1,0:T(8,128)S(1)}, u32[]{:S(2)}, u32[]{:S(2)}) collective-permute-start(f32[2,32,48,128]{3,2,1,0:T(8,128)S(1)} %bitcast.120), channel_id=1, source_target_pairs={{0,1},{1,2},{2,3},{3,4},{4,5},{5,6},{6,7},{7,8},{8,9},{9,10},{10,1... | collective-permute-start | bytes 4718600 | tf_op jit(solution)/shard_map/ppermute | solution.py:31
  324.1 80.6 %copy-start.2 = (f32[4,32,48,128]{3,2,1,0:T(8,128)S(1)}, f32[4,32,48,128]{3,2,1,0:T(8,128)}, u32[]{:S(2)}) copy-start(f32[4,32,48,128]{3,2,1,0:T(8,128)} %get-tuple-element.27) | copy-start | bytes 9437188
  403.0 1.6 copy-start.8
  919.0 1.8 copy-start.6
  920.7 45.9 %copy-start.5 = (f32[512,512]{1,0:T(8,128)}, f32[512,512]{1,0:T(8,128)S(1)}, u32[]{:S(2)}) copy-start(f32[512,512]{1,0:T(8,128)S(1)} %copy.55) | copy-start | bytes 3145732
  921.0 22.0 %copy-start.9 = (f32[512,512]{1,0:T(8,128)}, f32[512,512]{1,0:T(8,128)S(1)}, u32[]{:S(2)}) copy-start(f32[512,512]{1,0:T(8,128)S(1)} %fusion.64) | copy-start | bytes 3145732
  943.0 116.7 %copy-start.7 = (f32[512,512]{1,0:T(8,128)S(1)}, f32[512,512]{1,0:T(8,128)}, u32[]{:S(2)}) copy-start(f32[512,512]{1,0:T(8,128)} %fusion.77) | copy-start | bytes 3145732
Sparse Core Ops, SparseCore 0:
  613.6 305.3 all-reduce.2
